TPU v7x, 32 devices: a whole 2x2x4 slice. The times are simulated.
32 devices in a mesh: lat: 4 (over y, x), ma: 8 (over z, core).
Axes of the slice: x: 2, y: 2, z: 4, core: 2. Of those that a mesh axis runs over, the one named last changes fastest.
Arguments:
- fourier: bfloat16 [16, 2, 256, 2560], P(None, None, 'ma', 'lat'), may hold values from -6 to 6
- legendre: bfloat16 [16, 1280, 2, 640], P('ma', 'lat'), may hold values from -0.125 to 0.125
- window: int32 [16], replicated, may hold values from 0 to 639, as said below
- assign: int32 [16], replicated, may hold values from 0 to 15, each once
Outputs:
- coefficients: float32 [16, 2, 640, 256], P('ma', None, 'lat')
Inputs may be any that keep to these rules, and one draw needn't show every extreme that they name: `window`: distinct group numbers; 0 and 639 are always among them. `assign`: every position from 0 to 15 appears once.
All inputs are finite; a program needn't handle non-finite values.
Results may differ from a plain program's by a relative error of at most 0.017.
Values may be sent and summed in bfloat16 or wider, within the bound.
A program may use at most 64 MiB of HBM per device.

v0:
```python
import jax
import jax.numpy as jnp
from jax import lax
from jax.sharding import PartitionSpec as P


def swapped(value, axis, bit):
    mask = 2**bit
    pairs = [(source, source ^ mask) for source in range(lax.axis_size(axis))]
    return lax.ppermute(value, axis, pairs)


def fold_pairs(latitudes, northern):
    pair_rows = latitudes.shape[3] // 2
    leading_rows = latitudes[:, :, :, :pair_rows]
    trailing_rows = latitudes[:, :, :, pair_rows:]
    outgoing = jnp.where(northern, trailing_rows, leading_rows)
    bit_number = lax.axis_size("lat").bit_length() - 2
    arrived = swapped(outgoing, "lat", bit_number)
    staying = jnp.where(northern, leading_rows, trailing_rows)
    upper_rows = jnp.where(northern, staying, arrived).astype(jnp.float32)
    lower_rows = jnp.where(northern, arrived, staying).astype(jnp.float32)
    return (
        (upper_rows + lower_rows).astype(jnp.bfloat16),
        (upper_rows - lower_rows).astype(jnp.bfloat16),
    )


def on_device(fourier, legendre, window, assign):
    local_groups = legendre.shape[0]
    lat_count = lax.axis_size("lat")
    northern = lax.axis_index("lat") < lat_count // 2
    ordered = jnp.take(fourier, assign, axis=0)
    gathered = lax.all_to_all(ordered, "ma", split_axis=0, concat_axis=2, tiled=True)
    sym_part, anti_part = fold_pairs(gathered, northern)
    my_slots = lax.dynamic_slice_in_dim(assign, lax.axis_index("ma") * local_groups, local_groups)
    group_ids = jnp.take(window, my_slots)
    column_count = legendre.shape[3]
    wave_total = 2 * column_count
    zero_value = jnp.zeros((), jnp.bfloat16)

    def half_term(parity):
        column = 2 * lax.iota(jnp.int32, column_count) + parity
        upper_slot = (column[None, :] >= wave_total - group_ids[:, None])[:, None, :]
        table_part = legendre[:, :, parity, :]
        masked = jnp.stack(
            [
                jnp.where(upper_slot, zero_value, table_part),
                jnp.where(upper_slot, table_part, zero_value),
            ],
            axis=1,
        )
        leading = sym_part[:, 0] if parity == 0 else anti_part[:, 0]
        flipped = ((group_ids + parity) % 2 == 1)[:, None, None]
        trailing = jnp.where(flipped, anti_part[:, 1], sym_part[:, 1])
        sources = jnp.stack([leading, trailing], axis=1)
        return jnp.einsum("gspk,gsfp->gkf", masked, sources, preferred_element_type=jnp.float32)

    partials = jnp.stack([half_term(0), half_term(1)], axis=1)
    return lax.psum_scatter(
        partials.astype(jnp.bfloat16), "lat", scatter_dimension=2, tiled=True
    ).astype(jnp.float32)


def solution(mesh):
    return jax.shard_map(
        on_device,
        mesh=mesh,
        in_specs=(P(None, None, "ma", "lat"), P("ma", "lat", None, None), P(), P()),
        out_specs=P("ma", None, "lat", None),
        check_vma=False,
    )
```

profile of v0, /device:TPU:0, one launch (start us, length us, event | category | flops | bytes accessed | tf_op | source)
XLA Modules:
  0.0 113.9 jit_solution(5077408869157016032)
XLA Ops:
  6.5 0.8 compare_select_fusion
  7.3 0.7 compare_and_fusion
  8.0 0.8 gather_fusion.1
  8.8 1.3 %broadcast_select_fusion = bf16[16,2,32,640]{3,2,1,0:T(8,128)(2,1)} fusion(bf16[16,2,32,640]{3,2,1,0:T(8,128)(2,1)S(1)} %gather_fusion.1, pred[16]{0:T(512)(128)(4,1)S(1)} %compare_and_fusion), kind=kLoop, calls=%fused_computation.19 | loop fusion | flops 655360 | bytes 2621456 | tf_op jit(solution)/shard_map/jit(_take)/select_n | solution.py:33
  10.1 6.5 %all-to-all-start = ((bf16[16,2,32,640]{3,2,1,0:T(8,128)(2,1)}), bf16[16,2,32,640]{3,2,1,0:T(8,128)(2,1)}, u32[]{:S(2)}, u32[]{:S(2)}) async-start(bf16[16,2,32,640]{3,2,1,0:T(8,128)(2,1)} %broadcast_select_fusion), calls=%async_computation | async-start | bytes 2621440 | tf_op jit(solution)/shard_map/all_to_all | solution.py:34
  16.5 0.0 reduce-scatter.2.cloned.1.call-start
  16.6 0.1 compare_select_fusion.1
  16.7 0.6 gather_fusion
  17.3 0.1 fusion.34
  17.5 0.0 copy-done.2
  17.5 3.6 %fusion.40 = (bf16[2,320,1,640]{3,2,1,0:T(2,128)(2,1)}, bf16[2,320,1,640]{3,2,1,0:T(2,128)(2,1)}) fusion(bf16[2,320,2,640]{3,2,1,0:T(2,128)(2,1)S(1)} %copy-done.2), kind=kLoop, calls=%fused_computation.63 | loop fusion | bytes 3276800 | tf_op jit(solution)/shard_map/slice | solution.py:45
  21.0 27.8 %all-to-all-done = bf16[16,2,32,640]{3,2,1,0:T(8,128)(2,1)} async-done(((bf16[16,2,32,640]{3,2,1,0:T(8,128)(2,1)}), bf16[16,2,32,640]{3,2,1,0:T(8,128)(2,1)}, u32[]{:S(2)}, u32[]{:S(2)}) %all-to-all-start) | async-done | bytes 1310752 | tf_op jit(solution)/shard_map/all_to_all | solution.py:34
  48.9 1.4 %copy.15 = bf16[2,2,8,32,640]{4,3,2,1,0:T(8,128)(2,1)S(1)} copy(bf16[2,2,8,32,640]{4,3,1,0,2:T(8,128)(2,1)} %bitcast.2) | data formatting | bytes 2621440 | tf_op jit(solution)/shard_map/all_to_all | solution.py:34
  50.3 1.3 %fusion.41 = (bf16[2,2,256,320]{3,2,1,0:T(8,128)(2,1)}, bf16[2,2,256,320]{3,2,1,0:T(8,128)(2,1)S(1)}) fusion(bf16[2,2,256,640]{3,2,1,0:T(8,128)(2,1)S(1)} %bitcast.34), kind=kLoop, calls=%fused_computation.64 | loop fusion | bytes 2621440 | tf_op jit(solution)/shard_map/slice | solution.py:15
  51.6 1.1 copy.24
  52.7 2.4 %copy.23 = bf16[2,2,256,320]{2,3,1,0:T(8,128)(2,1)} copy(bf16[2,2,256,320]{3,2,1,0:T(8,128)(2,1)} %get-tuple-element.18) | data formatting | bytes 1310720
  55.1 1.3 %broadcast_select_fusion.7 = bf16[2,2,256,320]{2,3,1,0:T(8,128)(2,1)S(1)} fusion(bf16[2,2,256,320]{2,3,1,0:T(8,128)(2,1)} %copy.24, bf16[2,2,256,320]{2,3,1,0:T(8,128)(2,1)} %copy.23, pred[]{:T(512)S(6)} %lt.26), kind=kLoop, calls=%fused_computation.36 | loop fusion | flops 327680 | bytes 1966081 | tf_op jit(solution)/shard_map/jit(_where)/select_n | solution.py:17
  56.4 1.6 %collective-permute-start = (bf16[2,2,256,320]{2,3,1,0:T(8,128)(2,1)S(1)}, bf16[2,2,256,320]{2,3,1,0:T(8,128)(2,1)S(1)}, u32[]{:S(2)}, u32[]{:S(2)}) collective-permute-start(bf16[2,2,256,320]{2,3,1,0:T(8,128)(2,1)S(1)} %broadcast_select_fusion.7), channel_id=1, source_target_pairs={{0,16},{8,24},{16,0},{24,8},{1,17},{9,25},{17,1},{25,9},{2,18},{10... | collective-permute-start | bytes 1966088 | tf_op jit(solution)/shard_map/ppermute | solution.py:10
  58.0 0.1 broadcast_compare_fusion.1
  58.0 0.0 copy-done.4
  58.1 0.0 copy-start.5
  58.1 0.5 broadcast_select_fusion.2
  58.6 14.2 %collective-permute-done = bf16[2,2,256,320]{2,3,1,0:T(8,128)(2,1)S(1)} collective-permute-done((bf16[2,2,256,320]{2,3,1,0:T(8,128)(2,1)S(1)}, bf16[2,2,256,320]{2,3,1,0:T(8,128)(2,1)S(1)}, u32[]{:S(2)}, u32[]{:S(2)}) %collective-permute-start) | collective-permute-done | bytes 655392 | tf_op jit(solution)/shard_map/ppermute | solution.py:10
  72.7 0.4 fusion.21
  73.1 0.2 fusion.20
  73.3 0.2 broadcast_select_fusion.10
  73.5 0.8 fusion.22
  74.3 0.8 fusion.25
  75.1 1.2 %pad_maximum_fusion = bf16[2,2,640,256]{3,2,0,1:T(8,128)(2,1)} fusion(bf16[2,1,640,256]{3,2,0,1:T(8,128)(2,1)S(1)} %fusion.22, bf16[2,1,640,256]{3,2,0,1:T(8,128)(2,1)S(1)} %fusion.25), kind=kLoop, calls=%fused_computation.18 | loop fusion | flops 655360 | bytes 2621440 | tf_op jit(solution)/shard_map/stack | solution.py:59
  76.3 0.0 reduce-scatter.2.cloned.1.call-update
  76.4 28.8 %reduce-scatter.2.cloned.1.call-done = bf16[2,2,160,256]{3,2,0,1:T(8,128)(2,1)} async-done(((bf16[2,2,640,256]{3,2,0,1:T(8,128)(2,1)}), bf16[2,2,160,256]{3,2,0,1:T(8,128)(2,1)}) %reduce-scatter.2.cloned.1.call-update) | async-done | bytes 327696 | tf_op jit(solution)/shard_map/reduce_scatter | solution.py:60
  105.2 1.9 %copy.19 = f32[2,2,160,256]{3,2,1,0:T(8,128)} copy(bf16[2,2,160,256]{3,2,0,1:T(8,128)(2,1)} %reduce-scatter.2.cloned.1.call-done) | data formatting | bytes 983040 | tf_op jit(solution)/shard_map/convert_element_type | solution.py:62
  (19 shorter events, 0.1 us)
Async XLA Ops:
  6.5 1.4 %copy-start = (bf16[16,2,32,640]{3,2,1,0:T(8,128)(2,1)S(1)}, bf16[16,2,32,640]{3,2,1,0:T(8,128)(2,1)}, u32[]{:S(2)}) copy-start(bf16[16,2,32,640]{3,2,1,0:T(8,128)(2,1)} %param.4) | copy-start | bytes 3932164
  10.1 6.5 %copy-start.7 = (s32[16]{0:T(128)S(1)}, s32[16]{0:T(128)}, u32[]{:S(2)}) copy-start(s32[16]{0:T(128)} %param.7) | copy-start | bytes 196
  10.1 6.6 %copy-start.1 = (s32[16]{0:T(128)S(1)}, s32[16]{0:T(128)}, u32[]{:S(2)}) copy-start(s32[16]{0:T(128)} %param.6) | copy-start | bytes 196
  10.1 7.4 %copy-start.2 = (bf16[2,320,2,640]{3,2,1,0:T(2,128)(2,1)S(1)}, bf16[2,320,2,640]{3,2,1,0:T(2,128)(2,1)}, u32[]{:S(2)}) copy-start(bf16[2,320,2,640]{3,2,1,0:T(2,128)(2,1)} %param.5) | copy-start | bytes 4915204
  10.1 38.8 %all-to-all-start = ((bf16[16,2,32,640]{3,2,1,0:T(8,128)(2,1)}), bf16[16,2,32,640]{3,2,1,0:T(8,128)(2,1)}, u32[]{:S(2)}, u32[]{:S(2)}) async-start(bf16[16,2,32,640]{3,2,1,0:T(8,128)(2,1)} %broadcast_select_fusion), calls=%async_computation | async-start | bytes 2621440 | tf_op jit(solution)/shard_map/all_to_all | solution.py:34
  16.5 88.7 %reduce-scatter.2.cloned.1.call-start = ((), (), s32[]{:S(2)}) async-start(), calls=%async_computation.2 | async-start | bytes 1638400 | tf_op jit(solution)/shard_map/reduce_scatter | solution.py:60
  52.7 5.3 %copy-start.4 = (bf16[2,320,1,640]{3,2,1,0:T(2,128)(2,1)S(1)}, bf16[2,320,1,640]{3,2,1,0:T(2,128)(2,1)}, u32[]{:S(2)}) copy-start(bf16[2,320,1,640]{3,2,1,0:T(2,128)(2,1)} %get-tuple-element.15) | copy-start | bytes 2457604
  55.1 3.0 %copy-start.3 = (bf16[2,320,1,640]{3,2,1,0:T(2,128)(2,1)S(1)}, bf16[2,320,1,640]{3,2,1,0:T(2,128)(2,1)}, u32[]{:S(2)}) copy-start(bf16[2,320,1,640]{3,2,1,0:T(2,128)(2,1)} %get-tuple-element.14) | copy-start | bytes 2457604
  56.4 16.3 %collective-permute-start = (bf16[2,2,256,320]{2,3,1,0:T(8,128)(2,1)S(1)}, bf16[2,2,256,320]{2,3,1,0:T(8,128)(2,1)S(1)}, u32[]{:S(2)}, u32[]{:S(2)}) collective-permute-start(bf16[2,2,256,320]{2,3,1,0:T(8,128)(2,1)S(1)} %broadcast_select_fusion.7), channel_id=1, source_target_pairs={{0,16},{8,24},{16,0},{24,8},{1,17},{9,25},{17,1},{25,9},{2,18},{10... | collective-permute-start | bytes 1966088 | tf_op jit(solution)/shard_map/ppermute | solution.py:10
  58.1 14.7 %copy-start.5 = (bf16[2,2,256,320]{2,3,1,0:T(8,128)(2,1)S(1)}, bf16[2,2,256,320]{2,3,1,0:T(8,128)(2,1)}, u32[]{:S(2)}) copy-start(bf16[2,2,256,320]{2,3,1,0:T(8,128)(2,1)} %copy.24) | copy-start | bytes 1966084
  58.1 14.7 %copy-start.6 = (bf16[2,2,256,320]{2,3,1,0:T(8,128)(2,1)S(1)}, bf16[2,2,256,320]{2,3,1,0:T(8,128)(2,1)}, u32[]{:S(2)}) copy-start(bf16[2,2,256,320]{2,3,1,0:T(8,128)(2,1)} %copy.23) | copy-start | bytes 1966084
Sparse Core Ops, SparseCore 0:
  76.5 28.6 reduce-scatter.1
where the time goes:
time: 114 us
  waiting for transfers between devices  70.8 us (62%)
  between operations  13.5 us (12%)
  local copies, waits for them, and re-layouts  13.1 us (11%)
  starting transfers between devices  8.08 us (7%)
  other arithmetic  6.73 us (6%)
  matrix products  1.65 us (1%)
    reduce_scatter x1, waiting for transfers between devices, on_device(): lax.psum_scatter(partials.astype(jnp.bfloat16), 'lat', scatter_dimension=...  28.8 us
    all_to_all x1, waiting for transfers between devices, on_device(): lax.all_to_all(ordered, 'ma', split_axis=0, concat_axis=2, tiled=True)  27.8 us
    ppermute x1, waiting for transfers between devices, swapped(): return lax.ppermute(value, axis, pairs)  14.2 us
    all_to_all x1, starting transfers between devices, on_device(): lax.all_to_all(ordered, 'ma', split_axis=0, concat_axis=2, tiled=True)  6.46 us
    slice x1, local copies, waits for them, and re-layouts, half_term(): table_part = legendre[:, :, parity, :]  3.56 us
    unnamed x18, local copies, waits for them, and re-layouts  3.52 us
  transfers between devices with their start and end apart: 3, of which 3 were waited for; matrix products, arithmetic and copies ran while one was open for 4% of the time, Pallas kernels for 0%

commit v1 on v0

v1 whole, which is shorter than its diff:
```python
import functools

import jax
import jax.numpy as jnp
from jax import lax
from jax.experimental import pallas as pl
from jax.experimental.pallas import tpu as pltpu
from jax.sharding import PartitionSpec as P

MESH = pl.DeviceIdType.MESH
BF16 = jnp.bfloat16
F32 = jnp.float32


def swapped(value, axis, bit):
    mask = 2**bit
    pairs = [(source, source ^ mask) for source in range(lax.axis_size(axis))]
    return lax.ppermute(value, axis, pairs)


def fold_pairs(latitudes, northern):
    pair_rows = latitudes.shape[3] // 2
    leading_rows = latitudes[:, :, :, :pair_rows]
    trailing_rows = latitudes[:, :, :, pair_rows:]
    outgoing = jnp.where(northern, trailing_rows, leading_rows)
    bit_number = lax.axis_size("lat").bit_length() - 2
    arrived = swapped(outgoing, "lat", bit_number)
    staying = jnp.where(northern, leading_rows, trailing_rows)
    upper_rows = jnp.where(northern, staying, arrived).astype(F32)
    lower_rows = jnp.where(northern, arrived, staying).astype(F32)
    return (
        (upper_rows + lower_rows).astype(BF16),
        (upper_rows - lower_rows).astype(BF16),
    )


def plain_on_device(fourier, legendre, window, assign):
    local_groups = legendre.shape[0]
    lat_count = lax.axis_size("lat")
    northern = lax.axis_index("lat") < lat_count // 2
    count = assign.shape[0]
    chosen = assign[:, None] == lax.iota(jnp.int32, count)[None, :]
    ordered = jnp.einsum(
        "iw,wsfr->isfr", chosen.astype(BF16), fourier, preferred_element_type=F32
    ).astype(BF16)
    gathered = lax.all_to_all(ordered, "ma", split_axis=0, concat_axis=2, tiled=True)
    sym_part, anti_part = fold_pairs(gathered, northern)
    all_ids = jnp.sum(jnp.where(chosen, window[None, :], 0), axis=1)
    group_ids = lax.dynamic_slice_in_dim(
        all_ids, lax.axis_index("ma") * local_groups, local_groups
    )
    column_count = legendre.shape[3]
    wave_total = 2 * column_count
    zero_value = jnp.zeros((), BF16)

    def half_term(parity):
        column = 2 * lax.iota(jnp.int32, column_count) + parity
        upper_slot = (column[None, :] >= wave_total - group_ids[:, None])[:, None, :]
        table_part = legendre[:, :, parity, :]
        masked = jnp.stack(
            [
                jnp.where(upper_slot, zero_value, table_part),
                jnp.where(upper_slot, table_part, zero_value),
            ],
            axis=1,
        )
        leading = sym_part[:, 0] if parity == 0 else anti_part[:, 0]
        flipped = ((group_ids + parity) % 2 == 1)[:, None, None]
        trailing = jnp.where(flipped, anti_part[:, 1], sym_part[:, 1])
        sources = jnp.stack([leading, trailing], axis=1)
        return jnp.einsum("gspk,gsfp->gkf", masked, sources, preferred_element_type=F32)

    partials = jnp.stack([half_term(0), half_term(1)], axis=1)
    return lax.psum_scatter(
        partials.astype(BF16), "lat", scatter_dimension=2, tiled=True
    ).astype(F32)


def fused_kernel(
    lat_n,
    ma_n,
    assign_ref,
    window_ref,
    four_ref,
    leg_ref,
    out_ref,
    stage,
    recv,
    weight,
    part,
    landed,
    send_sem,
    recv_sem,
    psend_sem,
    precv_sem,
):
    groups_here = leg_ref.shape[0]
    fields_here = four_ref.shape[2]
    rows = four_ref.shape[3]
    pair = rows // 2
    body = pair // 128 * 128
    tail = pair - body
    kcols = leg_ref.shape[2]
    block = kcols // lat_n
    hemi = lat_n // 2
    half_ma = ma_n // 2
    half_f = half_ma * fields_here

    lat = lax.axis_index("lat")
    ma = lax.axis_index("ma")
    side = lat // hemi
    mine = side
    partner = lax.rem(lat + hemi, lat_n)
    my_half = ma // half_ma

    barrier = pltpu.get_barrier_semaphore()
    met = 0
    for r in range(ma_n):
        there = lax.rem(ma + r, ma_n)
        if r:
            pl.semaphore_signal(barrier, inc=1, device_id=(lat, there), device_id_type=MESH)
            met += 1
        pl.semaphore_signal(barrier, inc=1, device_id=(partner, there), device_id_type=MESH)
        met += 1
    for r in range(1, lat_n):
        if r != hemi:
            pl.semaphore_signal(
                barrier, inc=1, device_id=(lax.rem(lat + r, lat_n), ma), device_id_type=MESH
            )
            met += 1

    def pack(q, g):
        slab = four_ref.at[assign_ref[q * groups_here + g]]
        for t in range(2):
            a = slab[0, :, t * pair : (t + 1) * pair]
            b = slab[1, :, t * pair : (t + 1) * pair]
            stage[g, q, t] = jnp.concatenate(
                [a[:, :body], b[:, :body], a[:, body:], b[:, body:]], axis=1
            )

    def row_copy(g, q, own):
        t = mine if own else 1 - mine
        return pltpu.make_async_remote_copy(
            src_ref=stage.at[g, q, t],
            dst_ref=recv.at[g, side, ma],
            send_sem=send_sem.at[g, q, t],
            recv_sem=recv_sem.at[g, side, ma],
            device_id=(lat if own else partner, q),
            device_id_type=MESH,
        )

    def pack_all(g):
        def step(q, c):
            pack(q, g)
            return c

        lax.fori_loop(0, ma_n, step, 0)

    def send_all(g):
        def step(r, c):
            q = lax.rem(ma + half_ma + r, ma_n)
            row_copy(g, q, False).start()

            @pl.when(q != ma)
            def _():
                row_copy(g, q, True).start()

            return c

        lax.fori_loop(0, ma_n, step, 0)
        pltpu.make_async_copy(
            stage.at[g, ma, mine], recv.at[g, side, ma], recv_sem.at[g, side, ma]
        ).start()

    pack_all(0)
    pl.semaphore_wait(barrier, met)
    send_all(0)
    for g in range(1, groups_here):
        pack_all(g)
        send_all(g)

    ids = [window_ref[assign_ref[ma * groups_here + g]] for g in range(groups_here)]
    for g in range(groups_here):
        for e in range(2):

            def fill(j, c, g=g, e=e):
                start = pl.multiple_of(j * block, 16)
                table = leg_ref[g, e, pl.ds(start, block), :].astype(F32)
                k = start + lax.broadcasted_iota(jnp.int32, (block, 1), 0)
                low = 2 * k + e < 2 * kcols - ids[g]
                lower = jnp.where(low, table, 0.0)
                upper = jnp.where(low, 0.0, table)
                weight[g, e, pl.ds(start, block), :] = jnp.concatenate(
                    [lower[:, :body], upper[:, :body], lower[:, body:], upper[:, body:]],
                    axis=1,
                ).astype(BF16)
                return c

            lax.fori_loop(0, lat_n, fill, 0)

    lane = lax.broadcasted_iota(jnp.int32, (1, rows), 1)
    in_upper = ((lane >= body) & (lane < 2 * body)) | (lane >= 2 * body + tail)

    def part_copy(g, h, r):
        there = lax.rem(lat + r, lat_n)
        return pltpu.make_async_remote_copy(
            src_ref=part.at[g, h, there],
            dst_ref=landed.at[r - 1, g, h],
            send_sem=psend_sem.at[r - 1, g, h],
            recv_sem=precv_sem.at[r - 1, g, h],
            device_id=(there, ma),
            device_id_type=MESH,
        )

    def multiply(g, h):
        def arrive(m, c):
            for ns in range(2):
                piece = recv.at[g, ns, h * half_ma + m]
                pltpu.make_async_copy(piece, piece, recv_sem.at[g, ns, h * half_ma + m]).wait()
            return c

        lax.fori_loop(0, half_ma, arrive, 0)
        north = recv[g, 0, pl.ds(h * half_ma, half_ma)].reshape(half_f, rows).astype(F32)
        south = recv[g, 1, pl.ds(h * half_ma, half_ma)].reshape(half_f, rows).astype(F32)
        for e in range(2):
            odd = lax.rem(ids[g] + e, 2).astype(F32)
            sign = jnp.where(in_upper, 1.0 - 2.0 * odd, 1.0 - 2.0 * e)
            source = (north + sign * south).astype(BF16)
            for d in range(lat_n):
                part[g, h, d, e] = lax.dot_general(
                    weight[g, e, d * block : (d + 1) * block, :],
                    source,
                    (((1,), (1,)), ((), ())),
                    preferred_element_type=F32,
                ).astype(BF16)
        for r in range(1, lat_n):
            part_copy(g, h, r).start()

    def finish(g, h):
        for r in range(1, lat_n):
            part_copy(g, h, r).wait_recv()
        at = pl.multiple_of(h * half_f, 128)
        for e in range(2):
            total = part[g, h, lat, e].astype(F32)
            for r in range(1, lat_n):
                total = total + landed[r - 1, g, h, e].astype(F32)
            out_ref[g, e, :, pl.ds(at, half_f)] = total

    chunks = [(g, (my_half + j) % 2) for g in range(groups_here) for j in range(2)]
    for i, (g, h) in enumerate(chunks):
        multiply(g, h)
        if i:
            finish(*chunks[i - 1])
    finish(*chunks[-1])

    for g in range(groups_here):

        def sent(q, c, g=g):
            row_copy(g, q, False).wait_send()

            @pl.when(q != ma)
            def _():
                row_copy(g, q, True).wait_send()

            return c

        lax.fori_loop(0, ma_n, sent, 0)
    for g, h in chunks:
        for r in range(1, lat_n):
            part_copy(g, h, r).wait_send()


def fused_on_device(fourier, legendre, window, assign):
    lat_n, ma_n = lax.axis_size("lat"), lax.axis_size("ma")
    _, slots, fields_here, rows = fourier.shape
    groups_here, pair, parities, kcols = legendre.shape
    block = kcols // lat_n
    fields = fields_here * ma_n
    tables = jnp.transpose(legendre, (0, 2, 3, 1))
    vmem = pl.BlockSpec(memory_space=pltpu.VMEM)
    smem = pl.BlockSpec(memory_space=pltpu.SMEM)
    dma = pltpu.SemaphoreType.DMA
    return pl.pallas_call(
        functools.partial(fused_kernel, lat_n, ma_n),
        out_shape=jax.ShapeDtypeStruct((groups_here, 2, block, fields), F32),
        in_specs=[smem, smem, vmem, vmem],
        out_specs=vmem,
        scratch_shapes=[
            pltpu.VMEM((groups_here, ma_n, 2, fields_here, rows), BF16),
            pltpu.VMEM((groups_here, 2, ma_n, fields_here, rows), BF16),
            pltpu.VMEM((groups_here, 2, kcols, rows), BF16),
            pltpu.VMEM((groups_here, 2, lat_n, 2, block, fields // 2), BF16),
            pltpu.VMEM((lat_n - 1, groups_here, 2, 2, block, fields // 2), BF16),
            dma((groups_here, ma_n, 2)),
            dma((groups_here, 2, ma_n)),
            dma((lat_n - 1, groups_here, 2)),
            dma((lat_n - 1, groups_here, 2)),
        ],
        compiler_params=pltpu.CompilerParams(
            collective_id=0, has_side_effects=True, vmem_limit_bytes=40 * 2**20
        ),
        cost_estimate=pl.CostEstimate(
            flops=8 * groups_here * kcols * rows * fields,
            bytes_accessed=2 * (fourier.size + legendre.size),
            transcendentals=0,
        ),
    )(assign, window, fourier, tables)


def fits_kernel(mesh, fourier, legendre):
    lat_n, ma_n = mesh.shape["lat"], mesh.shape["ma"]
    fields_here = fourier.shape[2] // ma_n
    pair = legendre.shape[1] // lat_n
    block = legendre.shape[3] // lat_n
    return (
        fourier.shape[1] == 2
        and lat_n == 4
        and ma_n == 8
        and fields_here % 16 == 0
        and (fields_here * ma_n) % 256 == 0
        and (2 * pair) % 128 == 0
        and block % 16 == 0
    )


def solution(mesh):
    def run(fourier, legendre, window, assign):
        fused = fits_kernel(mesh, fourier, legendre)
        return jax.shard_map(
            fused_on_device if fused else plain_on_device,
            mesh=mesh,
            in_specs=(P(None, None, "ma", "lat"), P("ma", "lat", None, None), P(), P()),
            out_specs=P("ma", None, "lat", None),
            check_vma=False,
        )(fourier, legendre, window, assign)

    return run
```

time: 114 us -> 49.7 us (0.44)
  waiting for transfers between devices: 70.8 us -> 0 us
  Pallas kernels: 0 us -> 42.7 us
  between operations: 13.5 us -> 0.04 us
  starting transfers between devices: 8.08 us -> 0 us
  other arithmetic: 6.73 us -> 0 us
  local copies, waits for them, and re-layouts: 13.1 us -> 6.72 us
  matrix products: 1.65 us -> 0 us
    pallas_call x0 -> x1, Pallas kernels: none -> 42.7 us  [fused_on_device(): pl.pallas_call(functools.partial(fused_kernel, lat_n, ma_n), out_shape=ja...]
    reduce_scatter x1 -> x0, waiting for transfers between devices: 28.8 us -> none  [on_device(): lax.psum_scatter(partials.astype(jnp.bfloat16), 'lat', scatter_dimension=...]
    all_to_all x1 -> x0, waiting for transfers between devices: 27.8 us -> none  [on_device(): lax.all_to_all(ordered, 'ma', split_axis=0, concat_axis=2, tiled=True)]
    ppermute x1 -> x0, waiting for transfers between devices: 14.2 us -> none  [swapped(): return lax.ppermute(value, axis, pairs)]
    all_to_all x1 -> x0, starting transfers between devices: 6.46 us -> none  [on_device(): lax.all_to_all(ordered, 'ma', split_axis=0, concat_axis=2, tiled=True)]
    slice x2 -> x0, local copies, waits for them, and re-layouts: 4.83 us -> none  [the longest x1 3.56 us: half_term(): table_part = legendre[:, :, parity, :]]
    select_n x6 -> x0, other arithmetic: 4.08 us -> none  [the longest x2 2.07 us: on_device(): ordered = jnp.take(fourier, assign, axis=0)]
    unnamed x18 -> x8, local copies, waits for them, and re-layouts: 3.52 us -> 6.72 us
  transfers between devices with their start and end apart: 3 -> 0, of which waited for: 3 -> 0; matrix products, arithmetic and copies ran while one was open for 4% -> 0% of each run, Pallas kernels for 0% -> 0%
where the time goes in v1:
time: 49.7 us; the launch traced here: 49.5 us
  Pallas kernels  42.7 us (86%)
  local copies, waits for them, and re-layouts  6.72 us (14%)
    pallas_call x1, Pallas kernels, fused_on_device(): pl.pallas_call(functools.partial(fused_kernel, lat_n, ma_n), out_shape=ja...  42.7 us
    unnamed x8, local copies, waits for them, and re-layouts  6.72 us

profile of v1, /device:TPU:0, one launch (start us, length us, event | category | flops | bytes accessed | tf_op | source)
XLA Modules:
  0.0 49.5 jit_solution(5322326516029936862)
XLA Ops:
  0.0 0.0 copy-start.1
  0.0 0.0 copy-start.2
  0.0 0.0 copy-start
  0.0 5.9 %copy.5 = bf16[2,320,2,640]{1,3,2,0:T(8,128)(2,1)S(1)} copy(bf16[2,320,2,640]{3,2,1,0:T(2,128)(2,1)} %param.5) | data formatting | bytes 3276800 | tf_op args[1]
  5.9 0.0 copy-done.1
  5.9 0.0 copy-done.2
  5.9 0.0 copy-done
  5.9 42.7 %shard_map.46 = f32[2,2,160,256]{3,2,1,0:T(8,128)S(1)} custom-call(s32[16]{0:T(128)S(1)} %copy-done.1, s32[16]{0:T(128)S(1)} %copy-done.2, bf16[16,2,32,640]{3,2,1,0:T(8,128)(2,1)S(1)} %copy-done, bf16[2,2,640,320]{3,2,1,0:T(8,128)(2,1)S(1)} %bitcast.1), custom_call_target="tpu_custom_call" | custom-call | flops 1677721600 | bytes 2949120 | tf_op jit(solution)/shard_map/pallas_call | solution.py:283
  48.7 0.8 %copy.7 = f32[2,2,160,256]{3,2,1,0:T(8,128)} copy(f32[2,2,160,256]{3,2,1,0:T(8,128)S(1)} %shard_map.46) | data formatting | bytes 1310720
Async XLA Ops:
  0.0 5.9 %copy-start.1 = (s32[16]{0:T(128)S(1)}, s32[16]{0:T(128)}, u32[]{:S(2)}) copy-start(s32[16]{0:T(128)} %assign_ref.1) | copy-start | bytes 196
  0.0 5.9 %copy-start.2 = (s32[16]{0:T(128)S(1)}, s32[16]{0:T(128)}, u32[]{:S(2)}) copy-start(s32[16]{0:T(128)} %window_ref.1) | copy-start | bytes 196
  0.0 5.9 %copy-start = (bf16[16,2,32,640]{3,2,1,0:T(8,128)(2,1)S(1)}, bf16[16,2,32,640]{3,2,1,0:T(8,128)(2,1)}, u32[]{:S(2)}) copy-start(bf16[16,2,32,640]{3,2,1,0:T(8,128)(2,1)} %four_ref.1) | copy-start | bytes 3932164

commit v2 on v1

--- a/solution.py
+++ b/solution.py
@@ -100,7 +100,7 @@
     pair = rows // 2
     body = pair // 128 * 128
     tail = pair - body
-    kcols = leg_ref.shape[2]
+    kcols = leg_ref.shape[3]
     block = kcols // lat_n
     hemi = lat_n // 2
     half_ma = ma_n // 2
@@ -184,19 +184,19 @@
         for e in range(2):
 
             def fill(j, c, g=g, e=e):
-                start = pl.multiple_of(j * block, 16)
-                table = leg_ref[g, e, pl.ds(start, block), :].astype(F32)
-                k = start + lax.broadcasted_iota(jnp.int32, (block, 1), 0)
+                start = pl.multiple_of(j * 128, 128)
+                table = leg_ref[g, :, e, pl.ds(start, 128)].astype(F32).T
+                k = start + lax.broadcasted_iota(jnp.int32, (128, 1), 0)
                 low = 2 * k + e < 2 * kcols - ids[g]
                 lower = jnp.where(low, table, 0.0)
                 upper = jnp.where(low, 0.0, table)
-                weight[g, e, pl.ds(start, block), :] = jnp.concatenate(
+                weight[g, e, pl.ds(start, 128), :] = jnp.concatenate(
                     [lower[:, :body], upper[:, :body], lower[:, body:], upper[:, body:]],
                     axis=1,
                 ).astype(BF16)
                 return c
 
-            lax.fori_loop(0, lat_n, fill, 0)
+            lax.fori_loop(0, kcols // 128, fill, 0)
 
     lane = lax.broadcasted_iota(jnp.int32, (1, rows), 1)
     in_upper = ((lane >= body) & (lane < 2 * body)) | (lane >= 2 * body + tail)
@@ -276,7 +276,6 @@
     groups_here, pair, parities, kcols = legendre.shape
     block = kcols // lat_n
     fields = fields_here * ma_n
-    tables = jnp.transpose(legendre, (0, 2, 3, 1))
     vmem = pl.BlockSpec(memory_space=pltpu.VMEM)
     smem = pl.BlockSpec(memory_space=pltpu.SMEM)
     dma = pltpu.SemaphoreType.DMA
@@ -304,7 +303,7 @@
             bytes_accessed=2 * (fourier.size + legendre.size),
             transcendentals=0,
         ),
-    )(assign, window, fourier, tables)
+    )(assign, window, fourier, legendre)
 
 
 def fits_kernel(mesh, fourier, legendre):
@@ -320,6 +319,7 @@
         and (fields_here * ma_n) % 256 == 0
         and (2 * pair) % 128 == 0
         and block % 16 == 0
+        and legendre.shape[3] % 128 == 0
     )
 
 

time: 49.7 us -> 47.8 us (0.962)
  local copies, waits for them, and re-layouts: 6.72 us -> 4.89 us
    unnamed x8 -> x9, local copies, waits for them, and re-layouts: 6.72 us -> 4.89 us
where the time goes in v2:
time: 47.8 us; the launch traced here: 47.6 us
  Pallas kernels  42.7 us (89%)
  local copies, waits for them, and re-layouts  4.89 us (10%)
    pallas_call x1, Pallas kernels, fused_on_device(): pl.pallas_call(functools.partial(fused_kernel, lat_n, ma_n), out_shape=ja...  42.7 us
    unnamed x9, local copies, waits for them, and re-layouts  4.89 us

profile of v2, /device:TPU:0, one launch (start us, length us, event | category | flops | bytes accessed | tf_op | source)
XLA Modules:
  0.0 47.6 jit_solution(17749125596043442790)
XLA Ops:
  0.0 0.0 copy-start
  0.0 1.4 %copy-done = bf16[2,320,2,640]{3,2,1,0:T(2,128)(2,1)S(1)} copy-done((bf16[2,320,2,640]{3,2,1,0:T(2,128)(2,1)S(1)}, bf16[2,320,2,640]{3,2,1,0:T(2,128)(2,1)}, u32[]{:S(2)}) %copy-start) | copy-done | bytes 1638424
  1.4 0.0 copy-start.1
  1.4 1.3 %copy-done.1 = bf16[16,2,32,640]{3,2,1,0:T(8,128)(2,1)S(1)} copy-done((bf16[16,2,32,640]{3,2,1,0:T(8,128)(2,1)S(1)}, bf16[16,2,32,640]{3,2,1,0:T(8,128)(2,1)}, u32[]{:S(2)}) %copy-start.1) | copy-done | bytes 1310744
  2.7 0.0 copy-start.2
  2.8 0.7 %copy-done.2 = s32[16]{0:T(128)S(1)} copy-done((s32[16]{0:T(128)S(1)}, s32[16]{0:T(128)}, u32[]{:S(2)}) %copy-start.2) | copy-done | bytes 88
  3.4 0.0 copy-start.3
  3.4 0.7 %copy-done.3 = s32[16]{0:T(128)S(1)} copy-done((s32[16]{0:T(128)S(1)}, s32[16]{0:T(128)}, u32[]{:S(2)}) %copy-start.3) | copy-done | bytes 88
  4.1 42.7 %shard_map.46 = f32[2,2,160,256]{3,2,1,0:T(8,128)S(1)} custom-call(s32[16]{0:T(128)S(1)} %copy-done.2, s32[16]{0:T(128)S(1)} %copy-done.3, bf16[16,2,32,640]{3,2,1,0:T(8,128)(2,1)S(1)} %copy-done.1, bf16[2,320,2,640]{3,2,1,0:T(2,128)(2,1)S(1)} %copy-done), custom_call_target="tpu_custom_call" | custom-call | flops 1677721600 | bytes 2949120 | tf_op jit(solution)/shard_map/pallas_call | solution.py:282
  46.8 0.8 %copy.6 = f32[2,2,160,256]{3,2,1,0:T(8,128)} copy(f32[2,2,160,256]{3,2,1,0:T(8,128)S(1)} %shard_map.46) | data formatting | bytes 1310720
Async XLA Ops:
  0.0 1.4 %copy-start = (bf16[2,320,2,640]{3,2,1,0:T(2,128)(2,1)S(1)}, bf16[2,320,2,640]{3,2,1,0:T(2,128)(2,1)}, u32[]{:S(2)}) copy-start(bf16[2,320,2,640]{3,2,1,0:T(2,128)(2,1)} %leg_ref.1) | copy-start | bytes 4915204
  1.4 1.3 %copy-start.1 = (bf16[16,2,32,640]{3,2,1,0:T(8,128)(2,1)S(1)}, bf16[16,2,32,640]{3,2,1,0:T(8,128)(2,1)}, u32[]{:S(2)}) copy-start(bf16[16,2,32,640]{3,2,1,0:T(8,128)(2,1)} %four_ref.1) | copy-start | bytes 3932164
  2.7 0.7 %copy-start.2 = (s32[16]{0:T(128)S(1)}, s32[16]{0:T(128)}, u32[]{:S(2)}) copy-start(s32[16]{0:T(128)} %assign_ref.1) | copy-start | bytes 196
  3.4 0.7 %copy-start.3 = (s32[16]{0:T(128)S(1)}, s32[16]{0:T(128)}, u32[]{:S(2)}) copy-start(s32[16]{0:T(128)} %window_ref.1) | copy-start | bytes 196

commit v3 on v2

--- a/solution.py
+++ b/solution.py
@@ -81,9 +81,11 @@
     ma_n,
     assign_ref,
     window_ref,
+    four_hbm,
+    leg_hbm,
+    out_ref,
     four_ref,
     leg_ref,
-    out_ref,
     stage,
     recv,
     weight,
@@ -93,6 +95,8 @@
     recv_sem,
     psend_sem,
     precv_sem,
+    leg_sem,
+    four_sem,
 ):
     groups_here = leg_ref.shape[0]
     fields_here = four_ref.shape[2]
@@ -112,6 +116,11 @@
     mine = side
     partner = lax.rem(lat + hemi, lat_n)
     my_half = ma // half_ma
+
+    rows_copy = pltpu.make_async_copy(four_hbm, four_ref, four_sem)
+    rows_copy.start()
+    table_copy = pltpu.make_async_copy(leg_hbm, leg_ref, leg_sem)
+    table_copy.start()
 
     barrier = pltpu.get_barrier_semaphore()
     met = 0
@@ -149,16 +158,12 @@
             device_id_type=MESH,
         )
 
-    def pack_all(g):
-        def step(q, c):
+    def pack_send(g):
+        def step(r, c):
+            hop = r // 2
+            half = lax.rem(my_half + 1 + r, 2)
+            q = half * half_ma + lax.rem(ma + hop, half_ma)
             pack(q, g)
-            return c
-
-        lax.fori_loop(0, ma_n, step, 0)
-
-    def send_all(g):
-        def step(r, c):
-            q = lax.rem(ma + half_ma + r, ma_n)
             row_copy(g, q, False).start()
 
             @pl.when(q != ma)
@@ -172,12 +177,11 @@
             stage.at[g, ma, mine], recv.at[g, side, ma], recv_sem.at[g, side, ma]
         ).start()
 
-    pack_all(0)
+    rows_copy.wait()
     pl.semaphore_wait(barrier, met)
-    send_all(0)
-    for g in range(1, groups_here):
-        pack_all(g)
-        send_all(g)
+    for g in range(groups_here):
+        pack_send(g)
+    table_copy.wait()
 
     ids = [window_ref[assign_ref[ma * groups_here + g]] for g in range(groups_here)]
     for g in range(groups_here):
@@ -278,13 +282,16 @@
     fields = fields_here * ma_n
     vmem = pl.BlockSpec(memory_space=pltpu.VMEM)
     smem = pl.BlockSpec(memory_space=pltpu.SMEM)
+    hbm = pl.BlockSpec(memory_space=pltpu.HBM)
     dma = pltpu.SemaphoreType.DMA
     return pl.pallas_call(
         functools.partial(fused_kernel, lat_n, ma_n),
         out_shape=jax.ShapeDtypeStruct((groups_here, 2, block, fields), F32),
-        in_specs=[smem, smem, vmem, vmem],
+        in_specs=[smem, smem, hbm, hbm],
         out_specs=vmem,
         scratch_shapes=[
+            pltpu.VMEM(fourier.shape, BF16),
+            pltpu.VMEM(legendre.shape, BF16),
             pltpu.VMEM((groups_here, ma_n, 2, fields_here, rows), BF16),
             pltpu.VMEM((groups_here, 2, ma_n, fields_here, rows), BF16),
             pltpu.VMEM((groups_here, 2, kcols, rows), BF16),
@@ -294,9 +301,11 @@
             dma((groups_here, 2, ma_n)),
             dma((lat_n - 1, groups_here, 2)),
             dma((lat_n - 1, groups_here, 2)),
+            dma,
+            dma,
         ],
         compiler_params=pltpu.CompilerParams(
-            collective_id=0, has_side_effects=True, vmem_limit_bytes=40 * 2**20
+            collective_id=0, has_side_effects=True, vmem_limit_bytes=63 * 2**20
         ),
         cost_estimate=pl.CostEstimate(
             flops=8 * groups_here * kcols * rows * fields,

time: 47.8 us -> 46 us (0.962)
  local copies, waits for them, and re-layouts: 4.89 us -> 1.98 us
  Pallas kernels: 42.7 us -> 43.8 us
    unnamed x9 -> x1, local copies, waits for them, and re-layouts: 4.89 us -> 1.98 us
    pallas_call x1, Pallas kernels: 42.7 us -> 43.8 us  [fused_on_device(): pl.pallas_call(functools.partial(fused_kernel, lat_n, ma_n), out_shape=ja...]
where the time goes in v3:
time: 46 us; the launch traced here: 45.8 us
  Pallas kernels  43.8 us (95%)
  local copies, waits for them, and re-layouts  1.98 us (4%)
    pallas_call x1, Pallas kernels, fused_on_device(): pl.pallas_call(functools.partial(fused_kernel, lat_n, ma_n), out_shape=ja...  43.8 us
    unnamed x1, local copies, waits for them, and re-layouts  1.98 us

profile of v3, /device:TPU:0, one launch (start us, length us, event | category | flops | bytes accessed | tf_op | source)
XLA Modules:
  0.0 45.8 jit_solution(15091974425060230963)
XLA Ops:
  0.0 43.8 %shard_map.46 = f32[2,2,160,256]{3,2,1,0:T(8,128)} custom-call(s32[16]{0:T(128)} %assign_ref.1, s32[16]{0:T(128)} %window_ref.1, bf16[16,2,32,640]{3,2,1,0:T(8,128)(2,1)} %four_hbm.1, bf16[2,320,2,640]{3,2,1,0:T(2,128)(2,1)} %leg_hbm.1), custom_call_target="tpu_custom_call" | custom-call | flops 1677721600 | bytes 2949120 | tf_op jit(solution)/shard_map/pallas_call | solution.py:287
  43.8 2.0 %copy.6 = f32[2,2,160,256]{3,2,1,0:T(8,128)} copy(f32[2,2,160,256]{3,2,1,0:T(8,128)} %shard_map.46) | data formatting | bytes 1310720

commit v4 on v3

--- a/solution.py
+++ b/solution.py
@@ -160,8 +160,8 @@
 
     def pack_send(g):
         def step(r, c):
-            hop = r // 2
-            half = lax.rem(my_half + 1 + r, 2)
+            hop = lax.rem(r, half_ma)
+            half = lax.rem(my_half + 1 + r // half_ma, 2)
             q = half * half_ma + lax.rem(ma + hop, half_ma)
             pack(q, g)
             row_copy(g, q, False).start()
@@ -250,7 +250,7 @@
                 total = total + landed[r - 1, g, h, e].astype(F32)
             out_ref[g, e, :, pl.ds(at, half_f)] = total
 
-    chunks = [(g, (my_half + j) % 2) for g in range(groups_here) for j in range(2)]
+    chunks = [(g, (my_half + 1 + j) % 2) for g in range(groups_here) for j in range(2)]
     for i, (g, h) in enumerate(chunks):
         multiply(g, h)
         if i:

time: 46 us -> 50.3 us (1.093)
  the two profiles are of different devices: /device:TPU:0 before, /device:TPU:11 now
where the time goes in v4:
time: 50.3 us; the launch traced here: 50.1 us
  Pallas kernels  48.1 us (96%)
  local copies, waits for them, and re-layouts  1.98 us (4%)
    pallas_call x1, Pallas kernels, fused_on_device(): pl.pallas_call(functools.partial(fused_kernel, lat_n, ma_n), out_shape=ja...  48.1 us
    unnamed x1, local copies, waits for them, and re-layouts  1.98 us

profile of v4, /device:TPU:11, one launch (start us, length us, event | category | flops | bytes accessed | tf_op | source)
XLA Modules:
  0.0 50.1 jit_solution(764661561449894215)
XLA Ops:
  0.0 48.1 %shard_map.46 = f32[2,2,160,256]{3,2,1,0:T(8,128)} custom-call(s32[16]{0:T(128)} %assign_ref.1, s32[16]{0:T(128)} %window_ref.1, bf16[16,2,32,640]{3,2,1,0:T(8,128)(2,1)} %four_hbm.1, bf16[2,320,2,640]{3,2,1,0:T(2,128)(2,1)} %leg_hbm.1), custom_call_target="tpu_custom_call" | custom-call | flops 1677721600 | bytes 2949120 | tf_op jit(solution)/shard_map/pallas_call | solution.py:287
  48.1 2.0 %copy.6 = f32[2,2,160,256]{3,2,1,0:T(8,128)} copy(f32[2,2,160,256]{3,2,1,0:T(8,128)} %shard_map.46) | data formatting | bytes 1310720

commit v5 on v3

--- a/solution.py
+++ b/solution.py
@@ -83,6 +83,7 @@
     window_ref,
     four_hbm,
     leg_hbm,
+    out_hbm,
     out_ref,
     four_ref,
     leg_ref,
@@ -97,6 +98,7 @@
     precv_sem,
     leg_sem,
     four_sem,
+    out_sem,
 ):
     groups_here = leg_ref.shape[0]
     fields_here = four_ref.shape[2]
@@ -205,13 +207,13 @@
     lane = lax.broadcasted_iota(jnp.int32, (1, rows), 1)
     in_upper = ((lane >= body) & (lane < 2 * body)) | (lane >= 2 * body + tail)
 
-    def part_copy(g, h, r):
+    def part_copy(g, h, e, r):
         there = lax.rem(lat + r, lat_n)
         return pltpu.make_async_remote_copy(
-            src_ref=part.at[g, h, there],
-            dst_ref=landed.at[r - 1, g, h],
-            send_sem=psend_sem.at[r - 1, g, h],
-            recv_sem=precv_sem.at[r - 1, g, h],
+            src_ref=part.at[g, h, there, e],
+            dst_ref=landed.at[r - 1, g, h, e],
+            send_sem=psend_sem.at[r - 1, g, h, e],
+            recv_sem=precv_sem.at[r - 1, g, h, e],
             device_id=(there, ma),
             device_id_type=MESH,
         )
@@ -237,18 +239,24 @@
                     (((1,), (1,)), ((), ())),
                     preferred_element_type=F32,
                 ).astype(BF16)
-        for r in range(1, lat_n):
-            part_copy(g, h, r).start()
+            for r in range(1, lat_n):
+                part_copy(g, h, e, r).start()
+
+    def out_copy(g, h, e):
+        at = pl.multiple_of(h * half_f, 128)
+        return pltpu.make_async_copy(
+            out_ref.at[g, e, h], out_hbm.at[g, e, :, pl.ds(at, half_f)], out_sem.at[g, e, h]
+        )
 
     def finish(g, h):
-        for r in range(1, lat_n):
-            part_copy(g, h, r).wait_recv()
-        at = pl.multiple_of(h * half_f, 128)
         for e in range(2):
+            for r in range(1, lat_n):
+                part_copy(g, h, e, r).wait_recv()
             total = part[g, h, lat, e].astype(F32)
             for r in range(1, lat_n):
                 total = total + landed[r - 1, g, h, e].astype(F32)
-            out_ref[g, e, :, pl.ds(at, half_f)] = total
+            out_ref[g, e, h] = total
+            out_copy(g, h, e).start()
 
     chunks = [(g, (my_half + j) % 2) for g in range(groups_here) for j in range(2)]
     for i, (g, h) in enumerate(chunks):
@@ -270,8 +278,10 @@
 
         lax.fori_loop(0, ma_n, sent, 0)
     for g, h in chunks:
-        for r in range(1, lat_n):
-            part_copy(g, h, r).wait_send()
+        for e in range(2):
+            for r in range(1, lat_n):
+                part_copy(g, h, e, r).wait_send()
+            out_copy(g, h, e).wait()
 
 
 def fused_on_device(fourier, legendre, window, assign):
@@ -280,7 +290,6 @@
     groups_here, pair, parities, kcols = legendre.shape
     block = kcols // lat_n
     fields = fields_here * ma_n
-    vmem = pl.BlockSpec(memory_space=pltpu.VMEM)
     smem = pl.BlockSpec(memory_space=pltpu.SMEM)
     hbm = pl.BlockSpec(memory_space=pltpu.HBM)
     dma = pltpu.SemaphoreType.DMA
@@ -288,8 +297,9 @@
         functools.partial(fused_kernel, lat_n, ma_n),
         out_shape=jax.ShapeDtypeStruct((groups_here, 2, block, fields), F32),
         in_specs=[smem, smem, hbm, hbm],
-        out_specs=vmem,
+        out_specs=hbm,
         scratch_shapes=[
+            pltpu.VMEM((groups_here, 2, 2, block, fields // 2), F32),
             pltpu.VMEM(fourier.shape, BF16),
             pltpu.VMEM(legendre.shape, BF16),
             pltpu.VMEM((groups_here, ma_n, 2, fields_here, rows), BF16),
@@ -299,10 +309,11 @@
             pltpu.VMEM((lat_n - 1, groups_here, 2, 2, block, fields // 2), BF16),
             dma((groups_here, ma_n, 2)),
             dma((groups_here, 2, ma_n)),
-            dma((lat_n - 1, groups_here, 2)),
-            dma((lat_n - 1, groups_here, 2)),
+            dma((lat_n - 1, groups_here, 2, 2)),
+            dma((lat_n - 1, groups_here, 2, 2)),
             dma,
             dma,
+            dma((groups_here, 2, 2)),
         ],
         compiler_params=pltpu.CompilerParams(
             collective_id=0, has_side_effects=True, vmem_limit_bytes=63 * 2**20

time: 46 us -> 45.5 us (0.989)
  no operation moved by 1% of the time
where the time goes in v5:
time: 45.5 us; the launch traced here: 45.4 us
  Pallas kernels  43.4 us (95%)
  local copies, waits for them, and re-layouts  1.98 us (4%)
    pallas_call x1, Pallas kernels, fused_on_device(): pl.pallas_call(functools.partial(fused_kernel, lat_n, ma_n), out_shape=ja...  43.4 us
    unnamed x1, local copies, waits for them, and re-layouts  1.98 us

profile of v5, /device:TPU:0, one launch (start us, length us, event | category | flops | bytes accessed | tf_op | source)
XLA Modules:
  0.0 45.4 jit_solution(5274923828384898636)
XLA Ops:
  0.0 43.4 %shard_map.46 = f32[2,2,160,256]{3,2,1,0:T(8,128)} custom-call(s32[16]{0:T(128)} %assign_ref.1, s32[16]{0:T(128)} %window_ref.1, bf16[16,2,32,640]{3,2,1,0:T(8,128)(2,1)} %four_hbm.1, bf16[2,320,2,640]{3,2,1,0:T(2,128)(2,1)} %leg_hbm.1), custom_call_target="tpu_custom_call" | custom-call | flops 1677721600 | bytes 2949120 | tf_op jit(solution)/shard_map/pallas_call | solution.py:296
  43.4 2.0 %copy.6 = f32[2,2,160,256]{3,2,1,0:T(8,128)} copy(f32[2,2,160,256]{3,2,1,0:T(8,128)} %shard_map.46) | data formatting | bytes 1310720

commit v6 on v5

--- a/solution.py
+++ b/solution.py
@@ -232,15 +232,16 @@
             odd = lax.rem(ids[g] + e, 2).astype(F32)
             sign = jnp.where(in_upper, 1.0 - 2.0 * odd, 1.0 - 2.0 * e)
             source = (north + sign * south).astype(BF16)
-            for d in range(lat_n):
+            for r in (*range(1, lat_n), 0):
+                d = lax.rem(lat + r, lat_n)
                 part[g, h, d, e] = lax.dot_general(
-                    weight[g, e, d * block : (d + 1) * block, :],
+                    weight[g, e, pl.ds(pl.multiple_of(d * block, 16), block), :],
                     source,
                     (((1,), (1,)), ((), ())),
                     preferred_element_type=F32,
                 ).astype(BF16)
-            for r in range(1, lat_n):
-                part_copy(g, h, e, r).start()
+                if r:
+                    part_copy(g, h, e, r).start()
 
     def out_copy(g, h, e):
         at = pl.multiple_of(h * half_f, 128)

time: 45.5 us -> 45.4 us (level)
  no operation moved by 1% of the time
where the time goes in v6:
time: 45.4 us; the launch traced here: 45.2 us
  Pallas kernels  43.2 us (95%)
  local copies, waits for them, and re-layouts  1.98 us (4%)
    pallas_call x1, Pallas kernels, fused_on_device(): pl.pallas_call(functools.partial(fused_kernel, lat_n, ma_n), out_shape=ja...  43.2 us
    unnamed x1, local copies, waits for them, and re-layouts  1.98 us

profile of v6, /device:TPU:0, one launch (start us, length us, event | category | flops | bytes accessed | tf_op | source)
XLA Modules:
  0.0 45.2 jit_solution(11613311416733262864)
XLA Ops:
  0.0 43.2 %shard_map.46 = f32[2,2,160,256]{3,2,1,0:T(8,128)} custom-call(s32[16]{0:T(128)} %assign_ref.1, s32[16]{0:T(128)} %window_ref.1, bf16[16,2,32,640]{3,2,1,0:T(8,128)(2,1)} %four_hbm.1, bf16[2,320,2,640]{3,2,1,0:T(2,128)(2,1)} %leg_hbm.1), custom_call_target="tpu_custom_call" | custom-call | flops 1677721600 | bytes 2949120 | tf_op jit(solution)/shard_map/pallas_call | solution.py:297
  43.2 2.0 %copy.6 = f32[2,2,160,256]{3,2,1,0:T(8,128)} copy(f32[2,2,160,256]{3,2,1,0:T(8,128)} %shard_map.46) | data formatting | bytes 1310720
